TPU v7x, 32 devices: a whole 2x2x4 slice. The times are simulated.
32 devices in a mesh: groups: 2 (over x), section: 16 (over z, y, core).
Axes of the slice: x: 2, y: 2, z: 4, core: 2. Of those that a mesh axis runs over, the one named last changes fastest.
Arguments:
- queries: bfloat16 [4096, 4096], P(('groups', 'section')), parts along dimension 0, may hold values from -400 to 400
- keys: bfloat16 [4096, 256], P(('groups', 'section')), parts along dimension 0, may hold values from -4 to 4
- values: bfloat16 [4096, 256], P(('groups', 'section')), parts along dimension 0, may hold values from -6 to 6
- windows: int32 [32], P('groups'), parts along dimension 0, may hold values from 0 to 1024, as said below
Outputs:
- attended: bfloat16 [4096, 4096], P(('groups', 'section')), parts along dimension 0
- log_total: float32 [4096, 32], P(('groups', 'section')), parts along dimension 0
There are 2 independent parts, one for each index of `groups`. A program takes and returns all parts, laid end to end along the dimension named above; each array names one. Nothing has to cross between parts.
Inputs may be any that keep to these rules, and one draw needn't show every extreme that they name: `windows`: the first slice's window is 0 and the last slice's window is 1024.
All inputs are finite; a program needn't handle non-finite values.
Results may differ from a plain program's by a relative error of at most 0.0055.
Values may be sent and summed in bfloat16 or wider, within the bound.
No kernel may reach another device: no remote copies, remote signals or barrier semaphores. Data moves between devices by JAX's collectives and lax.ppermute only.
A program may use at most 64 MiB of HBM per device.

v0:
```python
import functools
import math

import jax
import jax.numpy as jnp
from jax import lax
from jax.experimental import pallas as pl
from jax.experimental.pallas import tpu as pltpu
from jax.sharding import PartitionSpec as P

HD = 128
SCALE = HD ** (-0.5)
TO_EXP2 = SCALE * math.log2(math.e)
HIDDEN = -1e30
SUM_ROWS = 8
STATE_ROWS = HD + 2 * SUM_ROWS
TOP_ROW = HD + SUM_ROWS
TILE = 64
VMEM = pl.BlockSpec(memory_space=pltpu.VMEM)
SMALL = pltpu.CompilerParams(vmem_limit_bytes=1 << 20)
HBM = pl.BlockSpec(memory_space=pltpu.HBM)
MARK = (8, HD)
LAST = "last"


def shifted(block, axis, distance):
    size = lax.axis_size(axis)
    return lax.ppermute(block, axis, [(i, (i + distance) % size) for i in range(size)])


def swapped(block, axis):
    return lax.ppermute(block, axis, [(i ^ 1, i) for i in range(lax.axis_size(axis))])


def dot(left, right, dims):
    return lax.dot_general(left, right, (dims, ((), ())), preferred_element_type=jnp.float32)


def run_chunks(q_ref, blocks, flags, row_flags, state_in, state_out, s_buf, p_buf, outs):
    rows, width = q_ref.shape
    groups = blocks[0].shape[1] // (2 * HD)
    slots, keys, wide = s_buf.shape
    heads = wide // HD
    chunks = width // wide
    per_group = chunks // groups
    row_part = jnp.concatenate([row_flags] * heads, 0)
    ones = jnp.ones((2 * SUM_ROWS, keys), jnp.bfloat16)
    key_ext, value_ext = [], []
    for g in range(groups):
        key_rows = jnp.concatenate([b[:, g * HD : (g + 1) * HD] for b in blocks], 0)
        value_rows = jnp.concatenate(
            [b[:, (groups + g) * HD : (groups + g + 1) * HD] for b in blocks], 0
        )
        key_ext.append(jnp.concatenate([key_rows, flags], 1))
        value_ext.append(jnp.concatenate([value_rows.T, ones], 0))

    def score(c):
        parts = [q_ref[:, c * wide + h * HD : c * wide + (h + 1) * HD] for h in range(heads)]
        query_rows = jnp.concatenate([jnp.concatenate(parts, 0), row_part], 1)
        s_buf[c % slots] = dot(key_ext[c // per_group], query_rows, ((1,), (1,)))

    def weigh(c):
        slot, step = c % slots, wide
        tops, factors = [], []
        for j in range(0, wide, step):
            tiles = [
                (k, slice(j, j + step)) for k in range(0, keys, TILE)
            ]
            top = None
            for k, lanes in tiles:
                part = s_buf[slot, k : k + TILE, lanes].reshape(TILE // 8, 8, step)
                part = jnp.max(part, 0)
                top = part if top is None else jnp.maximum(top, part)
            top = jnp.max(top, 0, keepdims=True)
            if state_in is not None:
                old = state_in[TOP_ROW : TOP_ROW + 1, c * wide + j : c * wide + j + step]
                top = jnp.maximum(top, old)
                factors.append(jnp.exp2((old - top) * TO_EXP2))
            for k, lanes in tiles:
                weights = jnp.exp2((s_buf[slot, k : k + TILE, lanes] - top) * TO_EXP2)
                p_buf[slot, k : k + TILE, lanes] = weights.astype(jnp.bfloat16)
            tops.append(top)
        top = jnp.concatenate(tops, 1)
        return top, (jnp.concatenate(factors, 1) if factors else None)

    def sum_up(c, top, factor):
        lanes = slice(c * wide, (c + 1) * wide)
        summed = dot(value_ext[c // per_group], p_buf[c % slots], ((1,), (0,)))[:TOP_ROW]
        if factor is not None:
            summed = summed + state_in[0:TOP_ROW, lanes] * factor
        if outs is None:
            state_out[0:TOP_ROW, lanes] = summed
            state_out[TOP_ROW : TOP_ROW + 1, lanes] = top
        else:
            finish(summed, top, c, heads, *outs)

    held = {}
    for t in range(chunks + 2):
        if t < chunks:
            score(t)
        if 0 <= t - 1 < chunks:
            held[t - 1] = weigh(t - 1)
        if 0 <= t - 2 < chunks:
            sum_up(t - 2, *held.pop(t - 2))


def finish(summed, top, c, heads, out_ref, log_ref):
    total = summed[HD : HD + 1]
    result = summed[:HD] * (1.0 / total)
    logs = top * SCALE + jnp.log(total)
    first = c * heads
    for h in range(heads):
        lanes = slice(h * HD, (h + 1) * HD)
        out_ref[:, (first + h) * HD : (first + h + 1) * HD] = result[:, lanes].T.astype(
            out_ref.dtype
        )
    log_ref[first : first + heads, :] = jnp.concatenate(
        [logs[:, h * HD : (h + 1) * HD] for h in range(heads)], 0
    )


def lane_row(rows):
    lane = lax.broadcasted_iota(jnp.int32, (rows, HD), 1)
    row = lax.broadcasted_iota(jnp.int32, (rows, HD), 0)
    return lane, row


def lowest_of(mark_ref):
    return jnp.max(mark_ref[...]).astype(jnp.int32)


def near_kernel(axis, mark_in, q_ref, own, other, state_out, mark, s_buf, p_buf):
    me = lax.axis_index(axis)
    rows = own.shape[0]
    lowest = lowest_of(mark_in)
    mark[...] = mark_in[...]
    lane, row = lane_row(rows)
    first_seen = jnp.where((me & 1) == 1, lowest - (me - 1) * rows, rows)
    other_flags = jnp.where((lane == 0) & (row < first_seen), 1.0, 0.0)
    own_flags = jnp.where((lane == row) & (row > 0), 1.0, 0.0)
    flags = jnp.concatenate([other_flags, own_flags], 0).astype(jnp.bfloat16)
    row_flags = jnp.where((lane == 0) | (lane > row), HIDDEN, 0.0).astype(jnp.bfloat16)
    run_chunks(
        q_ref, [other, own], flags, row_flags, None, state_out, s_buf, p_buf, None
    )


def any_seen(distances, me, rows, lowest):
    starts = [(who - d) * rows for d in distances for who in (me, me ^ 1)]
    return functools.reduce(jnp.logical_or, [s + rows > lowest for s in starts]), starts


def finish_all(state, wide, out_ref, log_ref):
    for c in range(state.shape[1] // wide):
        lanes = slice(c * wide, (c + 1) * wide)
        top = state[TOP_ROW : TOP_ROW + 1, lanes]
        finish(state[0:TOP_ROW, lanes], top, c, wide // HD, out_ref, log_ref)


def write_out(buffers, results, sems):
    copy_all(
        [pltpu.make_async_copy(x, y, sems.at[i]) for i, (x, y) in enumerate(zip(buffers, results))]
    )


def far_kernel(axis, distances, later, mark_in, q_ref, *refs):
    me = lax.axis_index(axis)
    count = 2 * len(distances)
    blocks, state_in = refs[:count], refs[count]
    rows = blocks[0].shape[0]
    lowest = lowest_of(mark_in)
    needed, starts = any_seen(distances, me, rows, lowest)
    last = later == LAST
    refs = refs[count + 1 :]
    state_out, outs = None, None
    if last:
        out_hbm, log_hbm, s_buf, p_buf, out_buf, log_buf, sems = refs[2:]
        outs = (out_buf, log_buf)
    elif later:
        state_out, mark, out_hbm, log_hbm, s_buf, p_buf, out_buf, log_buf, sems = refs
    else:
        state_out, mark, s_buf, p_buf = refs
    if not last:
        mark[...] = mark_in[...]

    @pl.when(needed)
    def _():
        lane, row = lane_row(rows)
        flags = jnp.concatenate(
            [jnp.where((lane == 0) & (row + s < lowest), 1.0, 0.0) for s in starts], 0
        ).astype(jnp.bfloat16)
        row_flags = jnp.where(lane == 0, HIDDEN, 0.0).astype(jnp.bfloat16)
        run_chunks(q_ref, blocks, flags, row_flags, state_in, state_out, s_buf, p_buf, outs)
        if last:
            write_out((out_buf, log_buf), (out_hbm, log_hbm), sems)

    if not last:

        @pl.when(jnp.logical_not(needed))
        def _():
            state_out[...] = state_in[...]

    if later and not last:
        more, _ = any_seen(later, me, rows, lowest)

        @pl.when(jnp.logical_not(more))
        def _():
            finish_all(state_out, s_buf.shape[2], out_buf, log_buf)
            write_out((out_buf, log_buf), (out_hbm, log_hbm), sems)


def attend(kernel, mark, queries, blocks, state, later):
    rows, width = queries.shape
    heads = width // HD
    groups = blocks[0].shape[1] // (2 * HD)
    wide = HD * math.gcd(heads // groups, 4)
    keys = len(blocks) * rows
    operands = [mark, queries, *blocks, *state]
    in_specs = [VMEM] * len(operands)
    results = [
        jax.ShapeDtypeStruct((rows, width), jnp.bfloat16),
        jax.ShapeDtypeStruct((heads, rows), jnp.float32),
    ]
    states = [
        jax.ShapeDtypeStruct((STATE_ROWS, width), jnp.float32),
        jax.ShapeDtypeStruct(MARK, jnp.float32),
    ]
    scratch = [
        pltpu.VMEM((2, keys, wide), jnp.float32),
        pltpu.VMEM((2, keys, wide), jnp.bfloat16),
    ]
    at = 2 + len(blocks)
    out_shape, out_specs, aliases = states, [VMEM] * 2, {at: 0} if state else {}
    if later:
        scratch += [
            pltpu.VMEM((rows, width), jnp.bfloat16),
            pltpu.VMEM((heads, rows), jnp.float32),
            pltpu.SemaphoreType.DMA((2,)),
        ]
        if later == LAST:
            out_shape, out_specs, aliases = results, [HBM] * 2, {at + 1: 0, at + 2: 1}
            in_specs[at + 1 :] = [HBM] * 2
        else:
            out_shape, out_specs = states + results, [VMEM, VMEM, HBM, HBM]
    return pl.pallas_call(
        kernel,
        in_specs=in_specs,
        out_specs=out_specs,
        out_shape=out_shape,
        scratch_shapes=scratch,
        input_output_aliases=aliases,
        cost_estimate=pl.CostEstimate(
            flops=4 * keys * rows * width,
            bytes_accessed=rows * width * 2,
            transcendentals=keys * rows * heads,
        ),
        compiler_params=pltpu.CompilerParams(vmem_limit_bytes=12 << 20),
    )(*operands)


def copy_all(copies):
    for copy in copies:
        copy.start()
    for copy in copies:
        copy.wait()


def own_kernel(k_hbm, v_hbm, own_ref, sems):
    width = k_hbm.shape[1]
    copy_all(
        [
            pltpu.make_async_copy(k_hbm, own_ref.at[:, pl.ds(0, width)], sems.at[0]),
            pltpu.make_async_copy(v_hbm, own_ref.at[:, pl.ds(width, width)], sems.at[1]),
        ]
    )


def query_kernel(axis, win_hbm, q_hbm, mark_ref, q_ref, win_ref, sems):
    copy_all(
        [
            pltpu.make_async_copy(win_hbm, win_ref, sems.at[0]),
            pltpu.make_async_copy(q_hbm, q_ref, sems.at[1]),
        ]
    )
    me = lax.axis_index(axis)
    lowest = jnp.maximum(me * q_ref.shape[0] - win_ref[me], 0)
    mark_ref[...] = jnp.full(mark_ref.shape, lowest.astype(jnp.float32))


def fetch(kernel, sources, out_shape, scratch):
    return pl.pallas_call(
        kernel,
        in_specs=[HBM] * len(sources),
        out_specs=[VMEM] * len(out_shape),
        out_shape=out_shape,
        scratch_shapes=scratch + [pltpu.SemaphoreType.DMA((2,))],
        compiler_params=SMALL,
    )(*[pltpu.with_memory_space_constraint(x, pltpu.HBM) for x in sources])


def fetched(axis, queries, keys, values, windows):
    rows, width = keys.shape
    (own,) = fetch(
        own_kernel, [keys, values], [jax.ShapeDtypeStruct((rows, 2 * width), keys.dtype)], []
    )
    mark, queries = fetch(
        functools.partial(query_kernel, axis),
        [windows, queries],
        [
            jax.ShapeDtypeStruct(MARK, jnp.float32),
            jax.ShapeDtypeStruct(queries.shape, queries.dtype),
        ],
        [pltpu.SMEM(windows.shape, windows.dtype)],
    )
    return own, mark, queries


def tied(block, earlier):
    def kernel(block_ref, earlier_ref, out_ref):
        pass

    return pl.pallas_call(
        kernel,
        in_specs=[VMEM, VMEM],
        out_specs=VMEM,
        out_shape=jax.ShapeDtypeStruct(block.shape, block.dtype),
        input_output_aliases={0: 0},
        compiler_params=SMALL,
    )(block, earlier)


def on_device(queries, keys, values, windows):
    axis = "section"
    reach = lax.axis_size(axis) // 2
    own, mark, queries = fetched(axis, queries, keys, values, windows)
    other = swapped(own, axis)
    held = {4: shifted(own, axis, 4), 2: shifted(own, axis, 2)}
    state, mark = attend(
        functools.partial(near_kernel, axis), mark, queries, [own, other], [], None
    )
    state = [state]
    rounds = [
        [d for d in (first + 2, first) if d <= reach] for first in range(2, reach + 1, 4)
    ]
    for index, distances in enumerate(rounds):
        blocks = []
        for d in distances:
            held[d] = tied(held[d], mark)
            if d + 4 <= reach:
                held[d + 4] = shifted(held[d], axis, 4)
            blocks += [held[d], swapped(held[d], axis)]
        later = LAST if index == len(rounds) - 1 else None
        if index == len(rounds) - 2:
            later = rounds[-1]
        result = attend(
            functools.partial(far_kernel, axis, distances, later),
            mark,
            queries,
            blocks,
            state,
            later,
        )
        if later != LAST:
            mark = result[1]
            state = [result[0], *result[2:]]
    return result[0], result[1].T


def solution(mesh):
    placed = (
        P(("groups", "section"), None),
        P(("groups", "section"), None),
        P(("groups", "section"), None),
        P("groups"),
    )
    return jax.shard_map(
        on_device,
        mesh=mesh,
        in_specs=placed,
        out_specs=(P(("groups", "section"), None), P(("groups", "section"), None)),
        check_vma=False,
    )
```

profile of v0, /device:TPU:15, one launch (start us, length us, event | category | flops | bytes accessed | tf_op | source)
XLA Modules:
  0.0 25.9 jit_solution(5542810006570130645)
XLA Ops:
  0.6 0.9 %shard_map.60.own = bf16[128,512]{1,0:T(8,128)(2,1)S(1)} custom-call(bf16[128,256]{1,0:T(8,128)(2,1)} %k_hbm.1, bf16[128,256]{1,0:T(8,128)(2,1)} %v_hbm.1), custom_call_target="tpu_custom_call" | custom-call | tf_op jit(solution)/shard_map/pallas_call | solution.py:291
  1.5 0.7 %collective-permute-start = (bf16[128,512]{1,0:T(8,128)(2,1)S(1)}, bf16[128,512]{1,0:T(8,128)(2,1)S(1)}, u32[]{:S(2)}, u32[]{:S(2)}) collective-permute-start(bf16[128,512]{1,0:T(8,128)(2,1)S(1)} %shard_map.60.own), channel_id=1, source_target_pairs={{1,0},{0,1},{3,2},{2,3},{5,4},{4,5},{7,6},{6,7},{9,8},{8,9},{11,10... | collective-permute-start | bytes 393224 | tf_op jit(solution)/shard_map/ppermute | solution.py:32
  2.3 1.2 %collective-permute-start.3 = (bf16[128,512]{1,0:T(8,128)(2,1)S(1)}, bf16[128,512]{1,0:T(8,128)(2,1)S(1)}, u32[]{:S(2)}, u32[]{:S(2)}) collective-permute-start(bf16[128,512]{1,0:T(8,128)(2,1)S(1)} %shard_map.60.own), channel_id=1, source_target_pairs={{0,2},{1,3},{2,4},{3,5},{4,6},{5,7},{6,8},{7,9},{8,10},{9,11},{10,... | collective-permute-start | bytes 393224 | tf_op jit(solution)/shard_map/ppermute | solution.py:28
  3.5 1.3 %collective-permute-start.1 = (bf16[128,512]{1,0:T(8,128)(2,1)S(1)}, bf16[128,512]{1,0:T(8,128)(2,1)S(1)}, u32[]{:S(2)}, u32[]{:S(2)}) collective-permute-start(bf16[128,512]{1,0:T(8,128)(2,1)S(1)} %shard_map.60.own), channel_id=1, source_target_pairs={{0,4},{1,5},{2,6},{3,7},{4,8},{5,9},{6,10},{7,11},{8,12},{9,13},{1... | collective-permute-start | bytes 393224 | tf_op jit(solution)/shard_map/ppermute | solution.py:28
  4.8 1.2 %shard_map.59 = (f32[8,128]{1,0:T(8,128)S(1)}, bf16[128,4096]{1,0:T(8,128)(2,1)S(1)}) custom-call(s32[16]{0:T(128)} %win_hbm.1, bf16[128,4096]{1,0:T(8,128)(2,1)} %q_hbm.1), custom_call_target="tpu_custom_call" | custom-call | tf_op jit(solution)/shard_map/pallas_call | solution.py:291
  6.1 0.0 collective-permute-done.other
  6.1 1.8 %shard_map.61 = (f32[144,4096]{1,0:T(8,128)S(1)}, f32[8,128]{1,0:T(8,128)S(1)}) custom-call(f32[8,128]{1,0:T(8,128)S(1)} %get-tuple-element.12.mark_in, bf16[128,4096]{1,0:T(8,128)(2,1)S(1)} %get-tuple-element.13.q_ref, bf16[128,512]{1,0:T(8,128)(2,1)S(1)} %shard_map.60.own, bf16[128,512]{1,0:T(8,128)(2,1)S(1)} %collective-permute-done.other), custom_call_target="tpu_custom_call" | custom-call | flops 536870912 | bytes 1048576 | tf_op jit(solution)/shard_map/pallas_call | solution.py:245
  7.9 0.0 collective-permute-done.3.block_ref
  7.9 0.7 %collective-permute-start.4 = (bf16[128,512]{1,0:T(8,128)(2,1)S(1)}, bf16[128,512]{1,0:T(8,128)(2,1)S(1)}, u32[]{:S(2)}, u32[]{:S(2)}) collective-permute-start(bf16[128,512]{1,0:T(8,128)(2,1)S(1)} %shard_map.63.refs_2_), channel_id=1, source_target_pairs={{1,0},{0,1},{3,2},{2,3},{5,4},{4,5},{7,6},{6,7},{9,8},{8,9},{11,10... | collective-permute-start | bytes 393224 | tf_op jit(solution)/shard_map/ppermute | solution.py:32
  8.6 1.5 %collective-permute-done.1.block_ref = bf16[128,512]{1,0:T(8,128)(2,1)S(1)} collective-permute-done((bf16[128,512]{1,0:T(8,128)(2,1)S(1)}, bf16[128,512]{1,0:T(8,128)(2,1)S(1)}, u32[]{:S(2)}, u32[]{:S(2)}) %collective-permute-start.1) | collective-permute-done | bytes 131104 | tf_op jit(solution)/shard_map/ppermute | solution.py:28
  10.1 0.8 %collective-permute-start.2 = (bf16[128,512]{1,0:T(8,128)(2,1)S(1)}, bf16[128,512]{1,0:T(8,128)(2,1)S(1)}, u32[]{:S(2)}, u32[]{:S(2)}) collective-permute-start(bf16[128,512]{1,0:T(8,128)(2,1)S(1)} %shard_map.62.refs_0_), channel_id=1, source_target_pairs={{1,0},{0,1},{3,2},{2,3},{5,4},{4,5},{7,6},{6,7},{9,8},{8,9},{11,10... | collective-permute-start | bytes 393224 | tf_op jit(solution)/shard_map/ppermute | solution.py:32
  10.9 1.3 %collective-permute-start.7 = (bf16[128,512]{1,0:T(8,128)(2,1)S(1)}, bf16[128,512]{1,0:T(8,128)(2,1)S(1)}, u32[]{:S(2)}, u32[]{:S(2)}) collective-permute-start(bf16[128,512]{1,0:T(8,128)(2,1)S(1)} %shard_map.63.refs_2_), channel_id=1, source_target_pairs={{0,4},{1,5},{2,6},{3,7},{4,8},{5,9},{6,10},{7,11},{8,12},{9,13},{1... | collective-permute-start | bytes 393224 | tf_op jit(solution)/shard_map/ppermute | solution.py:28
  12.2 1.3 %collective-permute-start.5 = (bf16[128,512]{1,0:T(8,128)(2,1)S(1)}, bf16[128,512]{1,0:T(8,128)(2,1)S(1)}, u32[]{:S(2)}, u32[]{:S(2)}) collective-permute-start(bf16[128,512]{1,0:T(8,128)(2,1)S(1)} %shard_map.62.refs_0_), channel_id=1, source_target_pairs={{0,4},{1,5},{2,6},{3,7},{4,8},{5,9},{6,10},{7,11},{8,12},{9,13},{1... | collective-permute-start | bytes 393224 | tf_op jit(solution)/shard_map/ppermute | solution.py:28
  13.5 0.0 collective-permute-done.4.refs_3_
  13.5 0.0 collective-permute-done.2.refs_1_
  13.5 3.3 %shard_map.64 = (f32[144,4096]{1,0:T(8,128)S(1)}, f32[8,128]{1,0:T(8,128)S(1)}, bf16[128,4096]{1,0:T(8,128)(2,1)}, f32[32,128]{1,0:T(8,128)}) custom-call(f32[8,128]{1,0:T(8,128)S(1)} %get-tuple-element.14.earlier_ref.mark_in, bf16[128,4096]{1,0:T(8,128)(2,1)S(1)} %get-tuple-element.13.q_ref, ...), custom_call_target="tpu_custom_call", output_to_operand_aliasing={{0}: (6, {})} | custom-call | flops 1073741824 | bytes 1048576 | tf_op jit(solution)/shard_map/pallas_call | solution.py:245
  16.9 0.0 collective-permute-done.7.block_ref
  16.9 0.8 %collective-permute-start.8 = (bf16[128,512]{1,0:T(8,128)(2,1)S(1)}, bf16[128,512]{1,0:T(8,128)(2,1)S(1)}, u32[]{:S(2)}, u32[]{:S(2)}) collective-permute-start(bf16[128,512]{1,0:T(8,128)(2,1)S(1)} %shard_map.66.refs_2_), channel_id=1, source_target_pairs={{1,0},{0,1},{3,2},{2,3},{5,4},{4,5},{7,6},{6,7},{9,8},{8,9},{11,10... | collective-permute-start | bytes 393224 | tf_op jit(solution)/shard_map/ppermute | solution.py:32
  17.7 2.0 %collective-permute-done.5.block_ref = bf16[128,512]{1,0:T(8,128)(2,1)S(1)} collective-permute-done((bf16[128,512]{1,0:T(8,128)(2,1)S(1)}, bf16[128,512]{1,0:T(8,128)(2,1)S(1)}, u32[]{:S(2)}, u32[]{:S(2)}) %collective-permute-start.5) | collective-permute-done | bytes 131104 | tf_op jit(solution)/shard_map/ppermute | solution.py:28
  19.7 0.6 %collective-permute-start.6 = (bf16[128,512]{1,0:T(8,128)(2,1)S(1)}, bf16[128,512]{1,0:T(8,128)(2,1)S(1)}, u32[]{:S(2)}, u32[]{:S(2)}) collective-permute-start(bf16[128,512]{1,0:T(8,128)(2,1)S(1)} %shard_map.65.refs_0_), channel_id=1, source_target_pairs={{1,0},{0,1},{3,2},{2,3},{5,4},{4,5},{7,6},{6,7},{9,8},{8,9},{11,10... | collective-permute-start | bytes 393224 | tf_op jit(solution)/shard_map/ppermute | solution.py:32
  20.3 0.0 collective-permute-done.8.refs_3_
  20.3 1.0 %collective-permute-done.6.refs_1_ = bf16[128,512]{1,0:T(8,128)(2,1)S(1)} collective-permute-done((bf16[128,512]{1,0:T(8,128)(2,1)S(1)}, bf16[128,512]{1,0:T(8,128)(2,1)S(1)}, u32[]{:S(2)}, u32[]{:S(2)}) %collective-permute-start.6) | collective-permute-done | bytes 131104 | tf_op jit(solution)/shard_map/ppermute | solution.py:32
  21.3 4.7 %shard_map.67 = (bf16[128,4096]{1,0:T(8,128)(2,1)}, f32[32,128]{1,0:T(8,128)}) custom-call(f32[8,128]{1,0:T(8,128)S(1)} %get-tuple-element.16.earlier_ref.mark_in, bf16[128,4096]{1,0:T(8,128)(2,1)S(1)} %get-tuple-element.13.q_ref, bf16[128,512]{1,0:T(8,128)(2,1)S(1)} %shard_map.65.refs_0_, ...), custom_call_target="tpu_custom_call", output_to_operand_aliasing={{0}: (7, {}), {1}: (8, {})} | custom-call | flops 1073741824 | bytes 1048576 | tf_op jit(solution)/shard_map/pallas_call | solution.py:245
  (4 shorter events, 0.0 us)
Async XLA Ops:
  1.5 4.5 %collective-permute-start = (bf16[128,512]{1,0:T(8,128)(2,1)S(1)}, bf16[128,512]{1,0:T(8,128)(2,1)S(1)}, u32[]{:S(2)}, u32[]{:S(2)}) collective-permute-start(bf16[128,512]{1,0:T(8,128)(2,1)S(1)} %shard_map.60.own), channel_id=1, source_target_pairs={{1,0},{0,1},{3,2},{2,3},{5,4},{4,5},{7,6},{6,7},{9,8},{8,9},{11,10... | collective-permute-start | bytes 393224 | tf_op jit(solution)/shard_map/ppermute | solution.py:32
  2.3 5.6 %collective-permute-start.3 = (bf16[128,512]{1,0:T(8,128)(2,1)S(1)}, bf16[128,512]{1,0:T(8,128)(2,1)S(1)}, u32[]{:S(2)}, u32[]{:S(2)}) collective-permute-start(bf16[128,512]{1,0:T(8,128)(2,1)S(1)} %shard_map.60.own), channel_id=1, source_target_pairs={{0,2},{1,3},{2,4},{3,5},{4,6},{5,7},{6,8},{7,9},{8,10},{9,11},{10,... | collective-permute-start | bytes 393224 | tf_op jit(solution)/shard_map/ppermute | solution.py:28
  3.5 6.6 %collective-permute-start.1 = (bf16[128,512]{1,0:T(8,128)(2,1)S(1)}, bf16[128,512]{1,0:T(8,128)(2,1)S(1)}, u32[]{:S(2)}, u32[]{:S(2)}) collective-permute-start(bf16[128,512]{1,0:T(8,128)(2,1)S(1)} %shard_map.60.own), channel_id=1, source_target_pairs={{0,4},{1,5},{2,6},{3,7},{4,8},{5,9},{6,10},{7,11},{8,12},{9,13},{1... | collective-permute-start | bytes 393224 | tf_op jit(solution)/shard_map/ppermute | solution.py:28
  7.9 5.6 %collective-permute-start.4 = (bf16[128,512]{1,0:T(8,128)(2,1)S(1)}, bf16[128,512]{1,0:T(8,128)(2,1)S(1)}, u32[]{:S(2)}, u32[]{:S(2)}) collective-permute-start(bf16[128,512]{1,0:T(8,128)(2,1)S(1)} %shard_map.63.refs_2_), channel_id=1, source_target_pairs={{1,0},{0,1},{3,2},{2,3},{5,4},{4,5},{7,6},{6,7},{9,8},{8,9},{11,10... | collective-permute-start | bytes 393224 | tf_op jit(solution)/shard_map/ppermute | solution.py:32
  10.1 3.5 %collective-permute-start.2 = (bf16[128,512]{1,0:T(8,128)(2,1)S(1)}, bf16[128,512]{1,0:T(8,128)(2,1)S(1)}, u32[]{:S(2)}, u32[]{:S(2)}) collective-permute-start(bf16[128,512]{1,0:T(8,128)(2,1)S(1)} %shard_map.62.refs_0_), channel_id=1, source_target_pairs={{1,0},{0,1},{3,2},{2,3},{5,4},{4,5},{7,6},{6,7},{9,8},{8,9},{11,10... | collective-permute-start | bytes 393224 | tf_op jit(solution)/shard_map/ppermute | solution.py:32
  10.9 6.0 %collective-permute-start.7 = (bf16[128,512]{1,0:T(8,128)(2,1)S(1)}, bf16[128,512]{1,0:T(8,128)(2,1)S(1)}, u32[]{:S(2)}, u32[]{:S(2)}) collective-permute-start(bf16[128,512]{1,0:T(8,128)(2,1)S(1)} %shard_map.63.refs_2_), channel_id=1, source_target_pairs={{0,4},{1,5},{2,6},{3,7},{4,8},{5,9},{6,10},{7,11},{8,12},{9,13},{1... | collective-permute-start | bytes 393224 | tf_op jit(solution)/shard_map/ppermute | solution.py:28
  12.2 7.5 %collective-permute-start.5 = (bf16[128,512]{1,0:T(8,128)(2,1)S(1)}, bf16[128,512]{1,0:T(8,128)(2,1)S(1)}, u32[]{:S(2)}, u32[]{:S(2)}) collective-permute-start(bf16[128,512]{1,0:T(8,128)(2,1)S(1)} %shard_map.62.refs_0_), channel_id=1, source_target_pairs={{0,4},{1,5},{2,6},{3,7},{4,8},{5,9},{6,10},{7,11},{8,12},{9,13},{1... | collective-permute-start | bytes 393224 | tf_op jit(solution)/shard_map/ppermute | solution.py:28
  16.9 3.4 %collective-permute-start.8 = (bf16[128,512]{1,0:T(8,128)(2,1)S(1)}, bf16[128,512]{1,0:T(8,128)(2,1)S(1)}, u32[]{:S(2)}, u32[]{:S(2)}) collective-permute-start(bf16[128,512]{1,0:T(8,128)(2,1)S(1)} %shard_map.66.refs_2_), channel_id=1, source_target_pairs={{1,0},{0,1},{3,2},{2,3},{5,4},{4,5},{7,6},{6,7},{9,8},{8,9},{11,10... | collective-permute-start | bytes 393224 | tf_op jit(solution)/shard_map/ppermute | solution.py:32
  19.7 1.6 %collective-permute-start.6 = (bf16[128,512]{1,0:T(8,128)(2,1)S(1)}, bf16[128,512]{1,0:T(8,128)(2,1)S(1)}, u32[]{:S(2)}, u32[]{:S(2)}) collective-permute-start(bf16[128,512]{1,0:T(8,128)(2,1)S(1)} %shard_map.65.refs_0_), channel_id=1, source_target_pairs={{1,0},{0,1},{3,2},{2,3},{5,4},{4,5},{7,6},{6,7},{9,8},{8,9},{11,10... | collective-permute-start | bytes 393224 | tf_op jit(solution)/shard_map/ppermute | solution.py:32
where the time goes:
time: 26.1 us; the launch traced here: 25.9 us
  Pallas kernels  12 us (46%)
  starting transfers between devices  8.75 us (34%)
  waiting for transfers between devices  4.51 us (17%)
  between operations  0.7 us (3%)
    pallas_call x3, Pallas kernels, attend(): pl.pallas_call(kernel, in_specs=in_specs, out_specs=out_specs, out_shape=...  9.82 us
    ppermute x4, starting transfers between devices, shifted(): lax.ppermute(block, axis, [(i, (i + distance) % size) for i in range(size)])  5.13 us
    ppermute x5, starting transfers between devices, swapped(): lax.ppermute(block, axis, [(i ^ 1, i) for i in range(lax.axis_size(axis))])  3.62 us
    ppermute x4, waiting for transfers between devices, shifted(): lax.ppermute(block, axis, [(i, (i + distance) % size) for i in range(size)])  3.51 us
    pallas_call x2, Pallas kernels, fetch(): pl.pallas_call(kernel, in_specs=[HBM] * len(sources), out_specs=[VMEM] *...  2.13 us
    ppermute x5, waiting for transfers between devices, swapped(): lax.ppermute(block, axis, [(i ^ 1, i) for i in range(lax.axis_size(axis))])  0.99 us
  transfers between devices with their start and end apart: 9, of which 3 were waited for; matrix products, arithmetic and copies ran while one was open for 0% of the time, Pallas kernels for 25%

commit v1 on v0

--- a/solution.py
+++ b/solution.py
@@ -213,7 +213,7 @@
     rows, width = queries.shape
     heads = width // HD
     groups = blocks[0].shape[1] // (2 * HD)
-    wide = HD * math.gcd(heads // groups, 4)
+    wide = HD * math.gcd(heads // groups, 8 if later == LAST else 4)
     keys = len(blocks) * rows
     operands = [mark, queries, *blocks, *state]
     in_specs = [VMEM] * len(operands)

time: 26.1 us -> 26 us (level)
  the two profiles are of different devices: /device:TPU:15 before, /device:TPU:13 now
where the time goes in v1:
time: 26 us; the launch traced here: 25.8 us
  Pallas kernels  11.8 us (45%)
  starting transfers between devices  8.73 us (34%)
  waiting for transfers between devices  4.52 us (17%)
  between operations  0.7 us (3%)
    pallas_call x3, Pallas kernels, attend(): pl.pallas_call(kernel, in_specs=in_specs, out_specs=out_specs, out_shape=...  9.69 us
    ppermute x4, starting transfers between devices, shifted(): lax.ppermute(block, axis, [(i, (i + distance) % size) for i in range(size)])  5.13 us
    ppermute x5, starting transfers between devices, swapped(): lax.ppermute(block, axis, [(i ^ 1, i) for i in range(lax.axis_size(axis))])  3.6 us
    ppermute x4, waiting for transfers between devices, shifted(): lax.ppermute(block, axis, [(i, (i + distance) % size) for i in range(size)])  3.53 us
    pallas_call x2, Pallas kernels, fetch(): pl.pallas_call(kernel, in_specs=[HBM] * len(sources), out_specs=[VMEM] *...  2.13 us
    ppermute x5, waiting for transfers between devices, swapped(): lax.ppermute(block, axis, [(i ^ 1, i) for i in range(lax.axis_size(axis))])  0.99 us
  transfers between devices with their start and end apart: 9, of which 3 were waited for; matrix products, arithmetic and copies ran while one was open for 0% of the time, Pallas kernels for 25%

profile of v1, /device:TPU:13, one launch (start us, length us, event | category | flops | bytes accessed | tf_op | source)
XLA Modules:
  0.0 25.8 jit_solution(16939674339103311091)
XLA Ops:
  0.6 0.9 %shard_map.60.own = bf16[128,512]{1,0:T(8,128)(2,1)S(1)} custom-call(bf16[128,256]{1,0:T(8,128)(2,1)} %k_hbm.1, bf16[128,256]{1,0:T(8,128)(2,1)} %v_hbm.1), custom_call_target="tpu_custom_call" | custom-call | tf_op jit(solution)/shard_map/pallas_call | solution.py:291
  1.5 0.7 %collective-permute-start = (bf16[128,512]{1,0:T(8,128)(2,1)S(1)}, bf16[128,512]{1,0:T(8,128)(2,1)S(1)}, u32[]{:S(2)}, u32[]{:S(2)}) collective-permute-start(bf16[128,512]{1,0:T(8,128)(2,1)S(1)} %shard_map.60.own), channel_id=1, source_target_pairs={{1,0},{0,1},{3,2},{2,3},{5,4},{4,5},{7,6},{6,7},{9,8},{8,9},{11,10... | collective-permute-start | bytes 393224 | tf_op jit(solution)/shard_map/ppermute | solution.py:32
  2.3 1.2 %collective-permute-start.3 = (bf16[128,512]{1,0:T(8,128)(2,1)S(1)}, bf16[128,512]{1,0:T(8,128)(2,1)S(1)}, u32[]{:S(2)}, u32[]{:S(2)}) collective-permute-start(bf16[128,512]{1,0:T(8,128)(2,1)S(1)} %shard_map.60.own), channel_id=1, source_target_pairs={{0,2},{1,3},{2,4},{3,5},{4,6},{5,7},{6,8},{7,9},{8,10},{9,11},{10,... | collective-permute-start | bytes 393224 | tf_op jit(solution)/shard_map/ppermute | solution.py:28
  3.5 1.3 %collective-permute-start.1 = (bf16[128,512]{1,0:T(8,128)(2,1)S(1)}, bf16[128,512]{1,0:T(8,128)(2,1)S(1)}, u32[]{:S(2)}, u32[]{:S(2)}) collective-permute-start(bf16[128,512]{1,0:T(8,128)(2,1)S(1)} %shard_map.60.own), channel_id=1, source_target_pairs={{0,4},{1,5},{2,6},{3,7},{4,8},{5,9},{6,10},{7,11},{8,12},{9,13},{1... | collective-permute-start | bytes 393224 | tf_op jit(solution)/shard_map/ppermute | solution.py:28
  4.8 1.2 %shard_map.59 = (f32[8,128]{1,0:T(8,128)S(1)}, bf16[128,4096]{1,0:T(8,128)(2,1)S(1)}) custom-call(s32[16]{0:T(128)} %win_hbm.1, bf16[128,4096]{1,0:T(8,128)(2,1)} %q_hbm.1), custom_call_target="tpu_custom_call" | custom-call | tf_op jit(solution)/shard_map/pallas_call | solution.py:291
  6.1 0.0 collective-permute-done.other
  6.1 1.8 %shard_map.61 = (f32[144,4096]{1,0:T(8,128)S(1)}, f32[8,128]{1,0:T(8,128)S(1)}) custom-call(f32[8,128]{1,0:T(8,128)S(1)} %get-tuple-element.12.mark_in, bf16[128,4096]{1,0:T(8,128)(2,1)S(1)} %get-tuple-element.13.q_ref, bf16[128,512]{1,0:T(8,128)(2,1)S(1)} %shard_map.60.own, bf16[128,512]{1,0:T(8,128)(2,1)S(1)} %collective-permute-done.other), custom_call_target="tpu_custom_call" | custom-call | flops 536870912 | bytes 1048576 | tf_op jit(solution)/shard_map/pallas_call | solution.py:245
  7.9 0.0 collective-permute-done.3.block_ref
  7.9 0.7 %collective-permute-start.4 = (bf16[128,512]{1,0:T(8,128)(2,1)S(1)}, bf16[128,512]{1,0:T(8,128)(2,1)S(1)}, u32[]{:S(2)}, u32[]{:S(2)}) collective-permute-start(bf16[128,512]{1,0:T(8,128)(2,1)S(1)} %shard_map.63.refs_2_), channel_id=1, source_target_pairs={{1,0},{0,1},{3,2},{2,3},{5,4},{4,5},{7,6},{6,7},{9,8},{8,9},{11,10... | collective-permute-start | bytes 393224 | tf_op jit(solution)/shard_map/ppermute | solution.py:32
  8.6 1.5 %collective-permute-done.1.block_ref = bf16[128,512]{1,0:T(8,128)(2,1)S(1)} collective-permute-done((bf16[128,512]{1,0:T(8,128)(2,1)S(1)}, bf16[128,512]{1,0:T(8,128)(2,1)S(1)}, u32[]{:S(2)}, u32[]{:S(2)}) %collective-permute-start.1) | collective-permute-done | bytes 131104 | tf_op jit(solution)/shard_map/ppermute | solution.py:28
  10.1 0.8 %collective-permute-start.2 = (bf16[128,512]{1,0:T(8,128)(2,1)S(1)}, bf16[128,512]{1,0:T(8,128)(2,1)S(1)}, u32[]{:S(2)}, u32[]{:S(2)}) collective-permute-start(bf16[128,512]{1,0:T(8,128)(2,1)S(1)} %shard_map.62.refs_0_), channel_id=1, source_target_pairs={{1,0},{0,1},{3,2},{2,3},{5,4},{4,5},{7,6},{6,7},{9,8},{8,9},{11,10... | collective-permute-start | bytes 393224 | tf_op jit(solution)/shard_map/ppermute | solution.py:32
  10.9 1.3 %collective-permute-start.7 = (bf16[128,512]{1,0:T(8,128)(2,1)S(1)}, bf16[128,512]{1,0:T(8,128)(2,1)S(1)}, u32[]{:S(2)}, u32[]{:S(2)}) collective-permute-start(bf16[128,512]{1,0:T(8,128)(2,1)S(1)} %shard_map.63.refs_2_), channel_id=1, source_target_pairs={{0,4},{1,5},{2,6},{3,7},{4,8},{5,9},{6,10},{7,11},{8,12},{9,13},{1... | collective-permute-start | bytes 393224 | tf_op jit(solution)/shard_map/ppermute | solution.py:28
  12.2 1.3 %collective-permute-start.5 = (bf16[128,512]{1,0:T(8,128)(2,1)S(1)}, bf16[128,512]{1,0:T(8,128)(2,1)S(1)}, u32[]{:S(2)}, u32[]{:S(2)}) collective-permute-start(bf16[128,512]{1,0:T(8,128)(2,1)S(1)} %shard_map.62.refs_0_), channel_id=1, source_target_pairs={{0,4},{1,5},{2,6},{3,7},{4,8},{5,9},{6,10},{7,11},{8,12},{9,13},{1... | collective-permute-start | bytes 393224 | tf_op jit(solution)/shard_map/ppermute | solution.py:28
  13.5 0.0 collective-permute-done.4.refs_3_
  13.5 0.0 collective-permute-done.2.refs_1_
  13.5 3.3 %shard_map.64 = (f32[144,4096]{1,0:T(8,128)S(1)}, f32[8,128]{1,0:T(8,128)S(1)}, bf16[128,4096]{1,0:T(8,128)(2,1)}, f32[32,128]{1,0:T(8,128)}) custom-call(f32[8,128]{1,0:T(8,128)S(1)} %get-tuple-element.14.earlier_ref.mark_in, bf16[128,4096]{1,0:T(8,128)(2,1)S(1)} %get-tuple-element.13.q_ref, ...), custom_call_target="tpu_custom_call", output_to_operand_aliasing={{0}: (6, {})} | custom-call | flops 1073741824 | bytes 1048576 | tf_op jit(solution)/shard_map/pallas_call | solution.py:245
  16.9 0.0 collective-permute-done.7.block_ref
  16.9 0.8 %collective-permute-start.8 = (bf16[128,512]{1,0:T(8,128)(2,1)S(1)}, bf16[128,512]{1,0:T(8,128)(2,1)S(1)}, u32[]{:S(2)}, u32[]{:S(2)}) collective-permute-start(bf16[128,512]{1,0:T(8,128)(2,1)S(1)} %shard_map.66.refs_2_), channel_id=1, source_target_pairs={{1,0},{0,1},{3,2},{2,3},{5,4},{4,5},{7,6},{6,7},{9,8},{8,9},{11,10... | collective-permute-start | bytes 393224 | tf_op jit(solution)/shard_map/ppermute | solution.py:32
  17.7 2.0 %collective-permute-done.5.block_ref = bf16[128,512]{1,0:T(8,128)(2,1)S(1)} collective-permute-done((bf16[128,512]{1,0:T(8,128)(2,1)S(1)}, bf16[128,512]{1,0:T(8,128)(2,1)S(1)}, u32[]{:S(2)}, u32[]{:S(2)}) %collective-permute-start.5) | collective-permute-done | bytes 131104 | tf_op jit(solution)/shard_map/ppermute | solution.py:28
  19.7 0.6 %collective-permute-start.6 = (bf16[128,512]{1,0:T(8,128)(2,1)S(1)}, bf16[128,512]{1,0:T(8,128)(2,1)S(1)}, u32[]{:S(2)}, u32[]{:S(2)}) collective-permute-start(bf16[128,512]{1,0:T(8,128)(2,1)S(1)} %shard_map.65.refs_0_), channel_id=1, source_target_pairs={{1,0},{0,1},{3,2},{2,3},{5,4},{4,5},{7,6},{6,7},{9,8},{8,9},{11,10... | collective-permute-start | bytes 393224 | tf_op jit(solution)/shard_map/ppermute | solution.py:32
  20.3 0.0 collective-permute-done.8.refs_3_
  20.3 1.0 %collective-permute-done.6.refs_1_ = bf16[128,512]{1,0:T(8,128)(2,1)S(1)} collective-permute-done((bf16[128,512]{1,0:T(8,128)(2,1)S(1)}, bf16[128,512]{1,0:T(8,128)(2,1)S(1)}, u32[]{:S(2)}, u32[]{:S(2)}) %collective-permute-start.6) | collective-permute-done | bytes 131104 | tf_op jit(solution)/shard_map/ppermute | solution.py:32
  21.3 4.5 %shard_map.67 = (bf16[128,4096]{1,0:T(8,128)(2,1)}, f32[32,128]{1,0:T(8,128)}) custom-call(f32[8,128]{1,0:T(8,128)S(1)} %get-tuple-element.16.earlier_ref.mark_in, bf16[128,4096]{1,0:T(8,128)(2,1)S(1)} %get-tuple-element.13.q_ref, bf16[128,512]{1,0:T(8,128)(2,1)S(1)} %shard_map.65.refs_0_, ...), custom_call_target="tpu_custom_call", output_to_operand_aliasing={{0}: (7, {}), {1}: (8, {})} | custom-call | flops 1073741824 | bytes 1048576 | tf_op jit(solution)/shard_map/pallas_call | solution.py:245
  (4 shorter events, 0.0 us)
Async XLA Ops:
  1.5 4.5 %collective-permute-start = (bf16[128,512]{1,0:T(8,128)(2,1)S(1)}, bf16[128,512]{1,0:T(8,128)(2,1)S(1)}, u32[]{:S(2)}, u32[]{:S(2)}) collective-permute-start(bf16[128,512]{1,0:T(8,128)(2,1)S(1)} %shard_map.60.own), channel_id=1, source_target_pairs={{1,0},{0,1},{3,2},{2,3},{5,4},{4,5},{7,6},{6,7},{9,8},{8,9},{11,10... | collective-permute-start | bytes 393224 | tf_op jit(solution)/shard_map/ppermute | solution.py:32
  2.3 5.7 %collective-permute-start.3 = (bf16[128,512]{1,0:T(8,128)(2,1)S(1)}, bf16[128,512]{1,0:T(8,128)(2,1)S(1)}, u32[]{:S(2)}, u32[]{:S(2)}) collective-permute-start(bf16[128,512]{1,0:T(8,128)(2,1)S(1)} %shard_map.60.own), channel_id=1, source_target_pairs={{0,2},{1,3},{2,4},{3,5},{4,6},{5,7},{6,8},{7,9},{8,10},{9,11},{10,... | collective-permute-start | bytes 393224 | tf_op jit(solution)/shard_map/ppermute | solution.py:28
  3.5 6.6 %collective-permute-start.1 = (bf16[128,512]{1,0:T(8,128)(2,1)S(1)}, bf16[128,512]{1,0:T(8,128)(2,1)S(1)}, u32[]{:S(2)}, u32[]{:S(2)}) collective-permute-start(bf16[128,512]{1,0:T(8,128)(2,1)S(1)} %shard_map.60.own), channel_id=1, source_target_pairs={{0,4},{1,5},{2,6},{3,7},{4,8},{5,9},{6,10},{7,11},{8,12},{9,13},{1... | collective-permute-start | bytes 393224 | tf_op jit(solution)/shard_map/ppermute | solution.py:28
  7.9 5.6 %collective-permute-start.4 = (bf16[128,512]{1,0:T(8,128)(2,1)S(1)}, bf16[128,512]{1,0:T(8,128)(2,1)S(1)}, u32[]{:S(2)}, u32[]{:S(2)}) collective-permute-start(bf16[128,512]{1,0:T(8,128)(2,1)S(1)} %shard_map.63.refs_2_), channel_id=1, source_target_pairs={{1,0},{0,1},{3,2},{2,3},{5,4},{4,5},{7,6},{6,7},{9,8},{8,9},{11,10... | collective-permute-start | bytes 393224 | tf_op jit(solution)/shard_map/ppermute | solution.py:32
  10.1 3.5 %collective-permute-start.2 = (bf16[128,512]{1,0:T(8,128)(2,1)S(1)}, bf16[128,512]{1,0:T(8,128)(2,1)S(1)}, u32[]{:S(2)}, u32[]{:S(2)}) collective-permute-start(bf16[128,512]{1,0:T(8,128)(2,1)S(1)} %shard_map.62.refs_0_), channel_id=1, source_target_pairs={{1,0},{0,1},{3,2},{2,3},{5,4},{4,5},{7,6},{6,7},{9,8},{8,9},{11,10... | collective-permute-start | bytes 393224 | tf_op jit(solution)/shard_map/ppermute | solution.py:32
  10.9 6.0 %collective-permute-start.7 = (bf16[128,512]{1,0:T(8,128)(2,1)S(1)}, bf16[128,512]{1,0:T(8,128)(2,1)S(1)}, u32[]{:S(2)}, u32[]{:S(2)}) collective-permute-start(bf16[128,512]{1,0:T(8,128)(2,1)S(1)} %shard_map.63.refs_2_), channel_id=1, source_target_pairs={{0,4},{1,5},{2,6},{3,7},{4,8},{5,9},{6,10},{7,11},{8,12},{9,13},{1... | collective-permute-start | bytes 393224 | tf_op jit(solution)/shard_map/ppermute | solution.py:28
  12.2 7.5 %collective-permute-start.5 = (bf16[128,512]{1,0:T(8,128)(2,1)S(1)}, bf16[128,512]{1,0:T(8,128)(2,1)S(1)}, u32[]{:S(2)}, u32[]{:S(2)}) collective-permute-start(bf16[128,512]{1,0:T(8,128)(2,1)S(1)} %shard_map.62.refs_0_), channel_id=1, source_target_pairs={{0,4},{1,5},{2,6},{3,7},{4,8},{5,9},{6,10},{7,11},{8,12},{9,13},{1... | collective-permute-start | bytes 393224 | tf_op jit(solution)/shard_map/ppermute | solution.py:28
  16.9 3.4 %collective-permute-start.8 = (bf16[128,512]{1,0:T(8,128)(2,1)S(1)}, bf16[128,512]{1,0:T(8,128)(2,1)S(1)}, u32[]{:S(2)}, u32[]{:S(2)}) collective-permute-start(bf16[128,512]{1,0:T(8,128)(2,1)S(1)} %shard_map.66.refs_2_), channel_id=1, source_target_pairs={{1,0},{0,1},{3,2},{2,3},{5,4},{4,5},{7,6},{6,7},{9,8},{8,9},{11,10... | collective-permute-start | bytes 393224 | tf_op jit(solution)/shard_map/ppermute | solution.py:32
  19.7 1.6 %collective-permute-start.6 = (bf16[128,512]{1,0:T(8,128)(2,1)S(1)}, bf16[128,512]{1,0:T(8,128)(2,1)S(1)}, u32[]{:S(2)}, u32[]{:S(2)}) collective-permute-start(bf16[128,512]{1,0:T(8,128)(2,1)S(1)} %shard_map.65.refs_0_), channel_id=1, source_target_pairs={{1,0},{0,1},{3,2},{2,3},{5,4},{4,5},{7,6},{6,7},{9,8},{8,9},{11,10... | collective-permute-start | bytes 393224 | tf_op jit(solution)/shard_map/ppermute | solution.py:32
